TPU v7x, 128 devices: a whole 4x4x4 slice. The times are simulated.
128 devices in a mesh: row: 16 (over y_lo, z, core), col: 8 (over x, y_hi).
Axes of the slice: x: 4, y: 4 (y_hi: 2, y_lo: 2; y = y_hi * 2 + y_lo), z: 4, core: 2. Of those that a mesh axis runs over, the one named last changes fastest.
Arguments:
- alignment: bfloat16 [256, 32768], P('row', 'col'), may hold values from -6 to 6
- pair_state: float32 [512, 512, 128], P('row', 'col'), may hold values from -6 to 6
- alignment_factor_weight: bfloat16 [64, 64], replicated, may hold values from -0.75 to 0.75
- outer_proj: bfloat16 [1024, 128], replicated, may hold values from -3 to 3
- outgoing_proj: bfloat16 [128, 640], replicated, may hold values from -0.5 to 0.5
- outgoing_final: bfloat16 [128, 128], replicated, may hold values from -0.5 to 0.5
- incoming_proj: bfloat16 [128, 640], replicated, may hold values from -0.5 to 0.5
- incoming_final: bfloat16 [128, 128], replicated, may hold values from -0.5 to 0.5
Outputs:
- pair_result: float32 [512, 512, 128], P('row', 'col')
All inputs are finite; a program needn't handle non-finite values.
Results may differ from a plain program's by a relative error of at most 0.0065.
Values may be sent and summed in bfloat16 or wider, within the bound.
A program may use at most 128 MiB of HBM per device.

v0:
```python
import functools

import jax
import jax.numpy as jnp
from jax import lax
from jax.experimental import pallas as pl
from jax.experimental.pallas import tpu as pltpu
from jax.sharding import PartitionSpec as P

epsilon = 1e-05
MESH = pl.DeviceIdType.MESH
NR, NC = 16, 8
ND = NR * NC
BF, F32 = jnp.bfloat16, jnp.float32


def sigmoid(x):
    return 0.5 * jnp.tanh(0.5 * x) + 0.5


def position():
    r, c = lax.axis_index("row"), lax.axis_index("col")
    return r, c, c // 2, lax.rem(c, 2) * 2 + r // 8, lax.rem(r // 2, 4), lax.rem(r, 2)


def partner(where, step):
    _, _, x, y, z, core = where
    k = lax.rem(step * 107, ND)
    x = lax.rem(x + lax.rem(k // 2, 4), 4)
    y = lax.rem(y + lax.rem(k // 8, 4), 4)
    z = lax.rem(z + k // 32, 4)
    core = lax.rem(core + k, 2)
    return lax.rem(y, 2) * 8 + z * 2 + core, x * 2 + y // 2


def columns_normed(v):
    centred = v - jnp.mean(v, axis=0, keepdims=True)
    spread = jnp.mean(centred * centred, axis=0, keepdims=True)
    return centred * lax.rsqrt(spread + epsilon)


def exchange(where, source, target, sems):
    r, c = where[:2]
    me = r * NC + c

    def send(step, carry):
        rr, cc = partner(where, step)
        pltpu.make_async_remote_copy(
            source.at[rr * NC + cc],
            target.at[me],
            sems.at[0],
            sems.at[1],
            device_id=(rr, cc),
            device_id_type=MESH,
        ).start()
        return carry

    lax.fori_loop(1, ND, send, 0)
    target[me] = source[me]


def await_exchange(where, source, target, sems):
    pltpu.make_async_remote_copy(
        source.at[pl.ds(0, ND - 1)],
        target.at[pl.ds(0, ND - 1)],
        sems.at[0],
        sems.at[1],
        device_id=where[:2],
        device_id_type=MESH,
    ).wait()


def kernel(
    col_ref, row_ref, pair_ref, opm_w, out_w, out_f, in_w, in_f, result,
    col_all, row_all, row_t, outer, pair, gate, spread_l, spread_r, matrices,
    send1, got1, back1, mix1, send2, got2, back2, mix2, bsems, sems,
):
    where = position()
    r, c = where[:2]
    me = r * NC + c
    home = (r // 2 == c).astype(jnp.int32)
    bar = pltpu.get_barrier_semaphore()

    def greet(rr, cc):
        @pl.when(jnp.logical_or(rr != r, cc != c))
        def _():
            pl.semaphore_signal(bar, inc=1, device_id=(rr, cc), device_id_type=MESH)

    def greet_rows(k, carry):
        rr = lax.rem(r + k, NR)
        greet(rr, c)
        greet(rr, r // 2)
        return carry

    def greet_cols(k, carry):
        greet(r, lax.rem(c + k, NC))
        return carry

    lax.fori_loop(0, NR, greet_rows, 0)
    lax.fori_loop(1, NC, greet_cols, 0)
    pl.semaphore_wait(bar, (NR - 1) + (NC - 1) + NR - home)

    mine = pl.ds(pl.multiple_of(r * 16, 16), 16)

    def send_col(k, carry):
        pltpu.make_async_remote_copy(
            col_ref, col_all.at[mine], bsems.at[0], bsems.at[1],
            device_id=(lax.rem(r + k, NR), c), device_id_type=MESH,
        ).start()
        return carry

    def send_row(k, carry):
        half, cc = lax.rem(k, 2), lax.rem(c + k // 2, NC)
        rr = 2 * c + half

        @pl.when(jnp.logical_or(rr != r, cc != c))
        def _():
            pltpu.make_async_remote_copy(
                row_ref.at[half], row_all.at[mine], bsems.at[2], bsems.at[3],
                device_id=(rr, cc), device_id_type=MESH,
            ).start()

        return carry

    lax.fori_loop(0, NR, send_row, 0)
    lax.fori_loop(1, NR, send_col, 0)
    col_all[mine] = col_ref[...]

    @pl.when(home == 1)
    def _():
        row_all[mine] = row_ref[lax.rem(r, 2)]

    def turn(t, carry):
        block = jnp.concatenate([pair_ref[t], pair_ref[t + 16]], axis=0)
        pair[:, pl.ds(pl.multiple_of(t * 128, 128), 128)] = block.T
        return carry

    lax.fori_loop(0, 16, turn, 0)

    @pl.when(home == 1)
    def _():
        part = pl.ds(0, 15 * 16)
        pltpu.make_async_remote_copy(
            row_all.at[part], row_all.at[part], bsems.at[2], bsems.at[3],
            device_id=(r, c), device_id_type=MESH,
        ).wait()

    @pl.when(home == 0)
    def _():
        pltpu.make_async_remote_copy(
            row_all, row_all, bsems.at[2], bsems.at[3],
            device_id=(r, c), device_id_type=MESH,
        ).wait()

    row_t[...] = row_all[...].T
    part = pl.ds(0, 15 * 16)
    pltpu.make_async_remote_copy(
        col_all.at[part], col_all.at[part], bsems.at[0], bsems.at[1],
        device_id=(r, c), device_id_type=MESH,
    ).wait()

    def outer_part(n, carry):
        at = pl.ds(pl.multiple_of(n * 256, 256), 256)
        outer[:, at] = jnp.dot(row_t[...], col_all[:, at], preferred_element_type=F32).astype(BF)
        return carry

    lax.fori_loop(0, 8, outer_part, 0)

    def opm(t2, carry):
        sides = []
        for k in range(2):
            t = t2 * 2 + k
            low = outer[pl.ds(pl.multiple_of(t * 32, 32), 32), :]
            high = outer[pl.ds(pl.multiple_of(t * 32 + 512, 32), 32), :]
            evens, odds = [], []
            for q in range(16):
                a, b = low[:, q * 128 : q * 128 + 128], high[:, q * 128 : q * 128 + 128]
                evens.append(jnp.concatenate([a[:, :64], b[:, :64]], axis=1))
                odds.append(jnp.concatenate([a[:, 64:], b[:, 64:]], axis=1))
            sides.append(jnp.concatenate(evens + odds, axis=0))
        term = jnp.dot(opm_w[...], jnp.concatenate(sides, axis=1), preferred_element_type=F32)
        at = pl.ds(pl.multiple_of(t2 * 256, 256), 256)
        pair[:, at] += term * (1.0 / 256.0)
        return carry

    lax.fori_loop(0, 8, opm, 0)

    def project(weights, send):
        def one(t2, carry):
            at = pl.ds(pl.multiple_of(t2 * 256, 256), 256)
            normed = columns_normed(pair[:, at]).astype(BF)
            p = jnp.dot(weights[...], normed, preferred_element_type=F32)
            left = sigmoid(p[:128]) * p[128:256]
            right = sigmoid(p[256:384]) * p[384:512]
            gate[:, at] = sigmoid(p[512:])
            for k in range(2):
                for b in range(16):
                    to = pl.ds(b * 128 + t2 * 2 + k, 8, stride=16)
                    spread_l[to, :] = left[b * 8 : b * 8 + 8, k * 128 : k * 128 + 128]
                    spread_r[to, :] = right[b * 8 : b * 8 + 8, k * 128 : k * 128 + 128]
            return carry

        lax.fori_loop(0, 8, one, 0)

        def pack(n, carry):
            at = pl.ds(pl.multiple_of(n * 256, 256), 256)
            to = pl.ds(pl.multiple_of(n * 16, 16), 16)
            send[to, 0] = spread_l[at, :].astype(BF).reshape(16, 16, 128)
            send[to, 1] = spread_r[at, :].astype(BF).reshape(16, 16, 128)
            return carry

        lax.fori_loop(0, 8, pack, 0)

    def mix(got, back, outgoing):
        for f in range(2):
            for m in range(4):
                def one(rr, carry, f=f, m=m):
                    a, b = got[rr * NC + 2 * m, f], got[rr * NC + 2 * m + 1, f]
                    for h in range(2):
                        s = slice(h * 64, h * 64 + 64)
                        to = pl.ds(pl.multiple_of(rr * 32 + h * 16, 16), 16)
                        matrices[f, to, m * 128 : m * 128 + 128] = jnp.concatenate(
                            [a[:, s], b[:, s]], axis=1
                        )
                    return carry

                lax.fori_loop(0, NR, one, 0)
        if outgoing:
            mixed = lax.dot_general(
                matrices[0], matrices[1], (((1,), (1,)), ((), ())), preferred_element_type=F32
            )
        else:
            mixed = lax.dot_general(
                matrices[0], matrices[1], (((0,), (0,)), ((), ())), preferred_element_type=F32
            )
        for rr in range(NR):
            low, high = mixed[rr * 32 : rr * 32 + 16], mixed[rr * 32 + 16 : rr * 32 + 32]
            for m in range(NC):
                s = slice(m * 64, m * 64 + 64)
                back[rr * NC + m] = jnp.concatenate([low[:, s], high[:, s]], axis=1).astype(BF)

    def finish(mixed, weights):
        v = mixed[...].astype(F32)
        spread_l[...] = columns_normed(v).reshape(2048, 128)

        def one(t2, carry):
            sides = []
            for k in range(2):
                sides.append(
                    jnp.concatenate(
                        [spread_l[pl.ds(b * 128 + t2 * 2 + k, 8, stride=16), :] for b in range(16)],
                        axis=0,
                    )
                )
            normed = jnp.concatenate(sides, axis=1).astype(BF)
            at = pl.ds(pl.multiple_of(t2 * 256, 256), 256)
            update = jnp.dot(weights[...], normed, preferred_element_type=F32)
            pair[:, at] += gate[:, at] * update
            return carry

        lax.fori_loop(0, 8, one, 0)

    for n, (weights, final, send, got, back, mixed) in enumerate((
        (out_w, out_f, send1, got1, back1, mix1),
        (in_w, in_f, send2, got2, back2, mix2),
    )):
        project(weights, send)
        exchange(where, send, got, sems.at[2 * n])
        await_exchange(where, send, got, sems.at[2 * n])
        mix(got, back, n == 0)
        exchange(where, back, mixed, sems.at[2 * n + 1])
        await_exchange(where, back, mixed, sems.at[2 * n + 1])
        finish(mixed, final)

    def turn_back(t, carry):
        block = pair[:, pl.ds(pl.multiple_of(t * 128, 128), 128)].T
        result[t] = block[:64]
        result[t + 16] = block[64:]
        return carry

    lax.fori_loop(0, 16, turn_back, 0)


def normalize_layer(values):
    average = jnp.mean(values, axis=-1, keepdims=True)
    centred = values - average
    spread = jnp.mean(centred * centred, axis=-1, keepdims=True)
    return centred * lax.rsqrt(spread + epsilon)


def local(
    alignment,
    pair_state,
    alignment_factor_weight,
    outer_proj,
    outgoing_proj,
    outgoing_final,
    incoming_proj,
    incoming_final,
):
    values = alignment.astype(F32).reshape(16, 64, 64)
    normed = normalize_layer(values).astype(BF)
    factors = jnp.dot(
        normed.reshape(1024, 64), alignment_factor_weight, preferred_element_type=F32
    ).astype(BF).reshape(16, 64, 64)
    row = factors[:, :, :32].reshape(16, 2, 1024).transpose(1, 0, 2)
    col = factors[:, :, 32:].transpose(0, 2, 1).reshape(16, 2048)
    opm_w = outer_proj.reshape(32, 16, 2, 128).transpose(3, 2, 1, 0).reshape(128, 1024)
    vmem = pl.BlockSpec(memory_space=pltpu.VMEM)
    v = pltpu.VMEM
    return pl.pallas_call(
        kernel,
        out_shape=jax.ShapeDtypeStruct((32, 64, 128), F32),
        in_specs=[vmem] * 8,
        out_specs=vmem,
        scratch_shapes=[
            v((256, 2048), BF), v((256, 1024), BF), v((1024, 256), BF), v((1024, 2048), BF),
            v((128, 2048), F32), v((128, 2048), F32), v((2048, 128), F32), v((2048, 128), F32),
            v((2, 512, 512), BF),
            v((128, 2, 16, 128), BF), v((128, 2, 16, 128), BF), v((128, 16, 128), BF), v((128, 16, 128), BF),
            v((128, 2, 16, 128), BF), v((128, 2, 16, 128), BF), v((128, 16, 128), BF), v((128, 16, 128), BF),
            pltpu.SemaphoreType.DMA((4,)),
            pltpu.SemaphoreType.DMA((4, 2)),
        ],
        compiler_params=pltpu.CompilerParams(
            collective_id=0, has_side_effects=True, vmem_limit_bytes=56 << 20
        ),
    )(
        col, row, pair_state, opm_w,
        outgoing_proj.T, outgoing_final.T, incoming_proj.T, incoming_final.T,
    )


def solution(mesh):
    return jax.shard_map(
        local,
        mesh=mesh,
        in_specs=(P("row", "col"), P("row", "col", None), P(), P(), P(), P(), P(), P()),
        out_specs=P("row", "col", None),
        check_vma=False,
    )
```

profile of v0, /device:TPU:1, one launch (start us, length us, event | category | flops | bytes accessed | tf_op | source)
XLA Modules:
  0.0 135.6 jit_solution(14603849550225646662)
XLA Ops:
  0.0 0.0 copy-start
  0.0 0.0 copy-start.4
  0.0 1.5 %copy.28 = bf16[128,128]{0,1:T(8,128)(2,1)} copy(bf16[128,128]{1,0:T(8,128)(2,1)} %param.13) | data formatting | bytes 65536 | tf_op args[5]
  1.5 0.0 copy-done.4
  1.5 0.0 copy-start.3
  1.5 0.7 copy.30
  2.2 0.0 copy-start.2
  2.2 1.8 %copy.27 = bf16[128,640]{0,1:T(8,128)(2,1)} copy(bf16[128,640]{1,0:T(8,128)(2,1)} %param.12) | data formatting | bytes 327680 | tf_op args[4]
  4.0 0.0 copy-done.3
  4.0 0.8 copy.29
  4.8 0.0 copy-done.2
  4.8 0.1 copy.26
  4.9 0.0 copy-start.1
  4.9 0.9 copy.31.opm_w
  5.8 0.0 copy-done.1
  5.8 0.2 reshape.48
  6.0 0.2 reduce_sum.18
  6.2 0.4 multiply_reduce_fusion
  6.6 0.1 div.9
  6.7 0.1 rsqrt.12
  6.8 0.2 reshape.47
  7.0 0.0 copy-done
  7.0 0.5 convolution_convert_fusion
  7.5 0.2 reshape.49
  7.7 0.2 copy.33
  8.0 0.3 reshape.51
  8.2 0.6 copy.37
  8.9 0.8 reshape.50.col_ref
  9.7 123.6 %shard_map.82 = f32[32,64,128]{2,1,0:T(8,128)} custom-call(bf16[16,2048]{1,0:T(8,128)(2,1)} %reshape.50.col_ref, bf16[2,16,1024]{2,1,0:T(8,128)(2,1)} %bitcast.21, f32[32,64,128]{2,1,0:T(8,128)} %pair_ref.1, bf16[128,1024]{1,0:T(8,128)(2,1)} %copy.31.opm_w, bf16[640,128]{1,0:T(8,128)(2,1)} %bitcast.18, bf16[128,128]{1,0:T(8,128)(2,1)} %bitcast.23, ...), custom_call_target="tpu_custom_call" | custom-call | tf_op jit(solution)/shard_map/pallas_call | solution.py:311
  133.3 2.3 %copy.39 = f32[32,64,128]{2,1,0:T(8,128)} copy(f32[32,64,128]{2,1,0:T(8,128)} %shard_map.82) | data formatting | bytes 2097152
  (4 shorter events, 0.1 us)
Async XLA Ops:
  0.0 7.0 %copy-start = (bf16[64,64]{1,0:T(8,128)(2,1)S(1)}, bf16[64,64]{1,0:T(8,128)(2,1)}, u32[]{:S(2)}) copy-start(bf16[64,64]{1,0:T(8,128)(2,1)} %param.10) | copy-start | bytes 24580
  0.0 1.5 %copy-start.4 = (bf16[128,128]{1,0:T(8,128)(2,1)S(1)}, bf16[128,128]{1,0:T(8,128)(2,1)}, u32[]{:S(2)}) copy-start(bf16[128,128]{1,0:T(8,128)(2,1)} %param.15) | copy-start | bytes 98308
  1.5 2.5 %copy-start.3 = (bf16[128,640]{1,0:T(8,128)(2,1)S(1)}, bf16[128,640]{1,0:T(8,128)(2,1)}, u32[]{:S(2)}) copy-start(bf16[128,640]{1,0:T(8,128)(2,1)} %param.14) | copy-start | bytes 491524
  2.2 2.6 %copy-start.2 = (bf16[1024,128]{1,0:T(8,128)(2,1)S(1)}, bf16[1024,128]{1,0:T(8,128)(2,1)}, u32[]{:S(2)}) copy-start(bf16[1024,128]{1,0:T(8,128)(2,1)} %param.11) | copy-start | bytes 786436
  4.9 0.9 copy-start.1
where the time goes:
time: 136 us
  Pallas kernels  124 us (91%)
  local copies, waits for them, and re-layouts  10.8 us (8%)
    pallas_call x1, Pallas kernels, local(): pl.pallas_call(kernel, out_shape=jax.ShapeDtypeStruct((32, 64, 128), F32)...  124 us
    unnamed x17, local copies, waits for them, and re-layouts  7.38 us

commit v1 on v0

v1 whole, which is shorter than its diff:
```python
import functools

import jax
import jax.numpy as jnp
from jax import lax
from jax.experimental import pallas as pl
from jax.experimental.pallas import tpu as pltpu
from jax.sharding import PartitionSpec as P

epsilon = 1e-05
MESH = pl.DeviceIdType.MESH
NR, NC = 16, 8
ND = NR * NC
BF, F32 = jnp.bfloat16, jnp.float32


def sigmoid(x):
    return 0.5 * jnp.tanh(0.5 * x) + 0.5


def position():
    return lax.axis_index("row"), lax.axis_index("col")


def columns_normed(v):
    centred = v - jnp.mean(v, axis=0, keepdims=True)
    spread = jnp.mean(centred * centred, axis=0, keepdims=True)
    return centred * lax.rsqrt(spread + epsilon)


def lanes(at, size):
    return pl.ds(pl.multiple_of(at * size, size), size)


def halves(a, b):
    return (
        jnp.concatenate([a[:, :64], b[:, :64]], axis=1),
        jnp.concatenate([a[:, 64:], b[:, 64:]], axis=1),
    )


def kernel(
    align_ref, factor_ref, pair_ref, opm_ref, out_w, out_f, in_w, in_f, result,
    row_send, col_all, row_all, row_t, outer, pair_in, pair, normed, gate, spread_l, spread_r,
    opm_w, weights, finals, matrices, turned, mixed,
    send1, got1, back1, mix1, send2, got2, back2, mix2, lsem, csems, bsems, sems,
):
    r, c = position()
    me = r * NC + c
    home = (r // 2 == c).astype(jnp.int32)
    bar = pltpu.get_barrier_semaphore()
    load_pair = pltpu.make_async_copy(pair_ref, pair_in, lsem)
    load_pair.start()

    def greet(rr, cc):
        @pl.when(jnp.logical_or(rr != r, cc != c))
        def _():
            pl.semaphore_signal(bar, inc=1, device_id=(rr, cc), device_id_type=MESH)

    def greet_rows(k, carry):
        rr = lax.rem(r + k, NR)
        greet(rr, c)
        greet(rr, r // 2)
        return carry

    def greet_cols(k, carry):
        greet(r, lax.rem(c + k, NC))
        return carry

    lax.fori_loop(0, NR, greet_rows, 0)
    lax.fori_loop(1, NC, greet_cols, 0)

    def by_token(g, carry):
        v = align_ref[:, lanes(g, 128)].astype(F32)
        w = pltpu.roll(v, 64, 1)
        for h in range(2):
            spread_l[pl.ds(h * 512 + 2 * g, 8, stride=64), :] = v[h * 8 : h * 8 + 8]
            spread_l[pl.ds(h * 512 + 2 * g + 1, 8, stride=64), :] = w[h * 8 : h * 8 + 8]
        return carry

    lax.fori_loop(0, 32, by_token, 0, unroll=8)
    values = spread_l[0:1024, 0:64]
    centred = values - jnp.mean(values, axis=-1, keepdims=True)
    spread = jnp.mean(centred * centred, axis=-1, keepdims=True)
    tokens = (centred * lax.rsqrt(spread + epsilon)).astype(BF)
    spread_l[1024:2048, :] = jnp.dot(
        tokens, jnp.concatenate([factor_ref[:, :32]] * 4, axis=1), preferred_element_type=F32
    )
    cols = lax.dot_general(
        factor_ref[...].T, tokens, (((1,), (1,)), ((), ())), preferred_element_type=F32
    )
    for b in range(4):
        for s in range(8):
            spread_r[pl.ds(b * 64 + s, 8, stride=8), :] = cols[
                32 + b * 8 : 40 + b * 8, s * 128 : s * 128 + 128
            ]
    mine = lanes(r, 16)
    for q in range(16):
        a, b = halves(spread_r[q * 16 : q * 16 + 8, :], spread_r[q * 16 + 8 : q * 16 + 16, :])
        col_all[mine, q * 128 : q * 128 + 128] = jnp.concatenate([a, b], axis=0).astype(BF)
    lane = lax.broadcasted_iota(jnp.int32, (16, 128), 1)
    for n in range(16):
        piece = None
        for k in range(4):
            at = 1024 + n * 4 + k
            v = jnp.concatenate(
                [spread_l[pl.ds(at, 8, stride=128), :], spread_l[pl.ds(at + 64, 8, stride=128), :]], axis=0
            )
            piece = v if k == 0 else jnp.where(lane < 32 * k, piece, v)
        row_send[n // 8, :, n % 8 * 128 : n % 8 * 128 + 128] = piece.astype(BF)

    pl.semaphore_wait(bar, (NR - 1) + (NC - 1) + NR - home)

    def send_row(k, carry):
        half, cc = lax.rem(k, 2), lax.rem(c + k // 2, NC)
        rr = 2 * c + half

        @pl.when(jnp.logical_or(rr != r, cc != c))
        def _():
            pltpu.make_async_remote_copy(
                row_send.at[half], row_all.at[mine], bsems.at[0], bsems.at[1],
                device_id=(rr, cc), device_id_type=MESH,
            ).start()

        return carry

    sibling = r + 1 - 2 * lax.rem(r, 2)

    def col_copy(rr, at, send_sem, got_sem):
        block = col_all.at[lanes(at, 16)]
        return pltpu.make_async_remote_copy(
            block, block, send_sem, got_sem, device_id=(rr, c), device_id_type=MESH
        )

    for k in range(1, 8):
        col_copy(lax.rem(r + 2 * k, NR), r, csems.at[0], csems.at[1 + k]).start()
    col_copy(sibling, r, csems.at[9], csems.at[10]).start()
    lax.fori_loop(0, NR, send_row, 0)

    @pl.when(home == 1)
    def _():
        row_all[mine] = row_send[lax.rem(r, 2)]

    for n, (w, f) in enumerate(((out_w, out_f), (in_w, in_f))):
        for b in range(5):
            weights[n, b] = w[:, b * 128 : b * 128 + 128].T
        finals[n] = f[...].T
    spread_l[0:1024, :] = opm_ref[...].astype(F32)
    for q in range(8):
        block = jnp.concatenate(
            [
                spread_l[pl.ds((q % 4 * 4 + k) * 2 + q // 4 + p * 256, 8, stride=32), :]
                for k in range(4)
                for p in range(4)
            ],
            axis=0,
        )
        opm_w[:, q * 128 : q * 128 + 128] = block.T.astype(BF)

    for k in range(1, 8):
        frm = lax.rem(r + 16 - 2 * k, NR)
        col_copy(r, frm, csems.at[0], csems.at[1 + k]).wait_recv()
        col_copy(sibling, frm, csems.at[9], csems.at[10]).start()

    load_pair.wait()

    def turn(t, carry):
        block = jnp.concatenate([pair_in[t], pair_in[t + 16]], axis=0)
        pair[:, lanes(t, 128)] = block.T
        return carry

    lax.fori_loop(0, 16, turn, 0)

    @pl.when(home == 1)
    def _():
        part = row_all.at[pl.ds(0, 15 * 16)]
        pltpu.make_async_remote_copy(
            part, part, bsems.at[0], bsems.at[1], device_id=(r, c), device_id_type=MESH
        ).wait()

    @pl.when(home == 0)
    def _():
        pltpu.make_async_remote_copy(
            row_all, row_all, bsems.at[0], bsems.at[1], device_id=(r, c), device_id_type=MESH
        ).wait()

    row_t[...] = row_all[...].T
    seven, eight = col_all.at[pl.ds(0, 7 * 16)], col_all.at[pl.ds(0, 8 * 16)]
    pltpu.make_async_remote_copy(
        seven, seven, csems.at[0], csems.at[1], device_id=(r, c), device_id_type=MESH
    ).wait_send()
    pltpu.make_async_remote_copy(
        eight, eight, csems.at[9], csems.at[10], device_id=(r, c), device_id_type=MESH
    ).wait()

    def outer_part(n, carry):
        at = lanes(n, 256)
        outer[:, at] = jnp.dot(row_t[...], col_all[:, at], preferred_element_type=F32).astype(BF)
        return carry

    lax.fori_loop(0, 8, outer_part, 0)

    def opm(t2, carry):
        sides = []
        for k in range(2):
            t = t2 * 2 + k
            low = outer[lanes(t, 32), :]
            high = outer[lanes(t + 16, 32), :]
            evens, odds = [], []
            for q in range(16):
                a, b = halves(low[:, q * 128 : q * 128 + 128], high[:, q * 128 : q * 128 + 128])
                evens.append(a)
                odds.append(b)
            sides.append(jnp.concatenate(evens + odds, axis=0))
        term = jnp.dot(opm_w[...], jnp.concatenate(sides, axis=1), preferred_element_type=F32)
        at = lanes(t2, 256)
        now = pair[:, at] + term * (1.0 / 256.0)
        pair[:, at] = now
        normed[:, at] = columns_normed(now).astype(BF)
        return carry

    lax.fori_loop(0, 8, opm, 0)

    def send_group(q, source, target, pairsems):
        def one(k, carry):
            rr, cc = q * 4 + k // NC, lax.rem(c + k, NC)

            @pl.when(jnp.logical_or(rr != r, cc != c))
            def _():
                pltpu.make_async_remote_copy(
                    source.at[rr * NC + cc], target.at[me], pairsems.at[0], pairsems.at[1],
                    device_id=(rr, cc), device_id_type=MESH,
                ).start()

            return carry

        lax.fori_loop(0, 32, one, 0)

    def await_all(source, target, pairsems):
        pltpu.make_async_remote_copy(
            source.at[pl.ds(0, ND - 1)], target.at[pl.ds(0, ND - 1)], pairsems.at[0], pairsems.at[1],
            device_id=(r, c), device_id_type=MESH,
        ).wait()

    def project(n, send, got, pairsems):
        def group(g, carry):
            q = lax.rem(r // 4 + g, 4)
            w = jnp.concatenate([weights[n, b, lanes(q, 32), :] for b in range(4)], axis=0)
            for m in range(4):
                p = jnp.dot(w, normed[:, m * 512 : m * 512 + 512], preferred_element_type=F32)
                left = sigmoid(p[:32]) * p[32:64]
                right = sigmoid(p[64:96]) * p[96:]
                for k in range(4):
                    for b in range(4):
                        to = pl.ds(b * 128 + m * 4 + k, 8, stride=16)
                        spread_l[to, :] = left[b * 8 : b * 8 + 8, k * 128 : k * 128 + 128]
                        spread_r[to, :] = right[b * 8 : b * 8 + 8, k * 128 : k * 128 + 128]
            to = lanes(q, 32)
            send[to, 0] = spread_l[0:512, :].astype(BF).reshape(32, 16, 128)
            send[to, 1] = spread_r[0:512, :].astype(BF).reshape(32, 16, 128)
            send_group(q, send, got, pairsems)
            return carry

        lax.fori_loop(0, 4, group, 0)
        got[me] = send[me]

        def gates(m, carry):
            at = lanes(m, 256)
            gate[:, at] = sigmoid(jnp.dot(weights[n, 4], normed[:, at], preferred_element_type=F32))
            return carry

        lax.fori_loop(0, 8, gates, 0)
        await_all(send, got, pairsems)

    def mix(n, got, back, target, pairsems):
        def place(rr, carry):
            for f in range(2):
                for m in range(4):
                    both = halves(got[rr * NC + 2 * m, f], got[rr * NC + 2 * m + 1, f])
                    for h in range(2):
                        to = pl.ds(pl.multiple_of(rr * 32 + h * 16, 16), 16)
                        matrices[f, to, m * 128 : m * 128 + 128] = both[h]
            return carry

        lax.fori_loop(0, NR, place, 0)
        turned[...] = matrices[1 - n].T

        def group(g, carry):
            q = lax.rem(r // 4 + g, 4)
            at = lanes(q, 128)
            left, right = (matrices[0, at, :], turned[...]) if n == 0 else (turned[at, :], matrices[1])
            mixed[...] = jnp.dot(left, right, preferred_element_type=F32)
            for k in range(4):
                for m in range(4):
                    s = slice(m * 128, m * 128 + 128)
                    both = halves(mixed[k * 32 : k * 32 + 16, s], mixed[k * 32 + 16 : k * 32 + 32, s])
                    for h in range(2):
                        back[(q * 4 + k) * NC + 2 * m + h] = both[h].astype(BF)
            send_group(q, back, target, pairsems)
            return carry

        lax.fori_loop(0, 4, group, 0)
        target[me] = back[me]
        await_all(back, target, pairsems)

    def finish(n, mixed):
        spread_l[...] = mixed[...].astype(F32).reshape(2048, 128)

        def one(t2, carry):
            sides = []
            for k in range(2):
                sides.append(
                    jnp.concatenate(
                        [spread_l[pl.ds(b * 128 + t2 * 2 + k, 8, stride=16), :] for b in range(16)],
                        axis=0,
                    )
                )
            v = columns_normed(jnp.concatenate(sides, axis=1)).astype(BF)
            at = lanes(t2, 256)
            now = pair[:, at] + gate[:, at] * jnp.dot(finals[n], v, preferred_element_type=F32)
            if n == 0:
                pair[:, at] = now
                normed[:, at] = columns_normed(now).astype(BF)
            else:
                for k in range(2):
                    block = now[:, k * 128 : k * 128 + 128].T
                    result[t2 * 2 + k] = block[:64]
                    result[t2 * 2 + k + 16] = block[64:]
            return carry

        lax.fori_loop(0, 8, one, 0)

    for n, (send, got, back, target) in enumerate(
        ((send1, got1, back1, mix1), (send2, got2, back2, mix2))
    ):
        project(n, send, got, sems.at[2 * n])
        mix(n, got, back, target, sems.at[2 * n + 1])
        finish(n, target)


def local(
    alignment,
    pair_state,
    alignment_factor_weight,
    outer_proj,
    outgoing_proj,
    outgoing_final,
    incoming_proj,
    incoming_final,
):
    vmem = pl.BlockSpec(memory_space=pltpu.VMEM)
    anywhere = pl.BlockSpec(memory_space=pl.ANY)
    v = pltpu.VMEM
    exchanged = [
        v((128, 2, 16, 128), BF), v((128, 2, 16, 128), BF), v((128, 16, 128), BF), v((128, 16, 128), BF),
    ]
    return pl.pallas_call(
        kernel,
        out_shape=jax.ShapeDtypeStruct((32, 64, 128), F32),
        in_specs=[vmem, vmem, anywhere] + [vmem] * 5,
        out_specs=vmem,
        scratch_shapes=[
            v((2, 16, 1024), BF), v((256, 2048), BF), v((256, 1024), BF), v((1024, 256), BF),
            v((1024, 2048), BF), v((32, 64, 128), F32), v((128, 2048), F32), v((128, 2048), BF),
            v((128, 2048), F32), v((2048, 128), F32), v((2048, 128), F32),
            v((128, 1024), BF), v((2, 5, 128, 128), BF), v((2, 128, 128), BF),
            v((2, 512, 512), BF), v((512, 512), BF), v((128, 512), F32),
            *exchanged, *exchanged,
            pltpu.SemaphoreType.DMA,
            pltpu.SemaphoreType.DMA((11,)),
            pltpu.SemaphoreType.DMA((2,)),
            pltpu.SemaphoreType.DMA((4, 2)),
        ],
        compiler_params=pltpu.CompilerParams(
            collective_id=0, has_side_effects=True, vmem_limit_bytes=56 << 20
        ),
    )(
        alignment, alignment_factor_weight, pair_state, outer_proj,
        outgoing_proj, outgoing_final, incoming_proj, incoming_final,
    )


def solution(mesh):
    return jax.shard_map(
        local,
        mesh=mesh,
        in_specs=(P("row", "col"), P("row", "col", None), P(), P(), P(), P(), P(), P()),
        out_specs=P("row", "col", None),
        check_vma=False,
    )
```

time: 136 us -> 100 us (0.74)
  Pallas kernels: 124 us -> 97.8 us
  local copies, waits for them, and re-layouts: 10.8 us -> 2.31 us
    pallas_call x1, Pallas kernels: 124 us -> 97.8 us  [local(): pl.pallas_call(kernel, out_shape=jax.ShapeDtypeStruct((32, 64, 128), F32)...]
    unnamed x17 -> x1, local copies, waits for them, and re-layouts: 7.38 us -> 2.31 us
    reshape x7 -> x0, local copies, waits for them, and re-layouts: 3.18 us -> none  [the longest x2 0.93 us: local(): row = factors[:, :, :32].reshape(16, 2, 1024).transpose(1, 0, 2)]
where the time goes in v1:
time: 100 us
  Pallas kernels  97.8 us (98%)
  local copies, waits for them, and re-layouts  2.31 us (2%)
    pallas_call x1, Pallas kernels, local(): pl.pallas_call(kernel, out_shape=jax.ShapeDtypeStruct((32, 64, 128), F32)...  97.8 us
    unnamed x1, local copies, waits for them, and re-layouts  2.31 us

profile of v1, /device:TPU:1, one launch (start us, length us, event | category | flops | bytes accessed | tf_op | source)
XLA Modules:
  0.0 100.2 jit_solution(11458030155219783730)
XLA Ops:
  0.0 97.8 %shard_map.82 = f32[32,64,128]{2,1,0:T(8,128)} custom-call(bf16[16,4096]{1,0:T(8,128)(2,1)} %align_ref.1, bf16[64,64]{1,0:T(8,128)(2,1)} %factor_ref.1, f32[32,64,128]{2,1,0:T(8,128)} %pair_ref.1, bf16[1024,128]{1,0:T(8,128)(2,1)} %opm_ref.1, bf16[128,640]{1,0:T(8,128)(2,1)} %out_w.1, bf16[128,128]{1,0:T(8,128)(2,1)} %out_f.1, bf16[128,640]{1,0:T(8,128)(2,1)} %in_w.1, ...), custom_call_target="tpu_custom_call" | custom-call | tf_op jit(solution)/shard_map/pallas_call | solution.py:357
  97.8 2.3 %copy.10 = f32[32,64,128]{2,1,0:T(8,128)} copy(f32[32,64,128]{2,1,0:T(8,128)} %shard_map.82) | data formatting | bytes 2097152

commit v2 on v1

--- a/solution.py
+++ b/solution.py
@@ -40,17 +40,26 @@
 
 
 def kernel(
-    align_ref, factor_ref, pair_ref, opm_ref, out_w, out_f, in_w, in_f, result,
-    row_send, col_all, row_all, row_t, outer, pair_in, pair, normed, gate, spread_l, spread_r,
+    align_hbm, factor_hbm, pair_hbm, opm_hbm, out_w_hbm, out_f_hbm, in_w_hbm, in_f_hbm, result,
+    align_ref, factor_ref, pair_in, opm_ref, out_w, out_f, in_w, in_f, row_send, col_all, row_all, row_t, outer, pair, normed, gate, spread_l, spread_r,
     opm_w, weights, finals, matrices, turned, mixed,
     send1, got1, back1, mix1, send2, got2, back2, mix2, lsem, csems, bsems, sems,
 ):
     r, c = position()
     me = r * NC + c
+    z, group_here = r // 2 % 4, r // 8 * 2 + r % 2
+    channel = group_here * 32 + z * NC + c
     home = (r // 2 == c).astype(jnp.int32)
     bar = pltpu.get_barrier_semaphore()
-    load_pair = pltpu.make_async_copy(pair_ref, pair_in, lsem)
-    load_pair.start()
+    loads = [
+        pltpu.make_async_copy(source, to, lsem.at[k])
+        for k, (source, to) in enumerate((
+            (align_hbm, align_ref), (factor_hbm, factor_ref), (pair_hbm, pair_in), (opm_hbm, opm_ref),
+            (out_w_hbm, out_w), (out_f_hbm, out_f), (in_w_hbm, in_w), (in_f_hbm, in_f),
+        ))
+    ]
+    for load in loads:
+        load.start()
 
     def greet(rr, cc):
         @pl.when(jnp.logical_or(rr != r, cc != c))
@@ -58,17 +67,20 @@
             pl.semaphore_signal(bar, inc=1, device_id=(rr, cc), device_id_type=MESH)
 
     def greet_rows(k, carry):
-        rr = lax.rem(r + k, NR)
+        rr = (r + k) & 15
         greet(rr, c)
         greet(rr, r // 2)
         return carry
 
     def greet_cols(k, carry):
-        greet(r, lax.rem(c + k, NC))
+        greet(r, (c + k) & 7)
         return carry
 
     lax.fori_loop(0, NR, greet_rows, 0)
     lax.fori_loop(1, NC, greet_cols, 0)
+
+    loads[0].wait()
+    loads[1].wait()
 
     def by_token(g, carry):
         v = align_ref[:, lanes(g, 128)].astype(F32)
@@ -112,7 +124,7 @@
     pl.semaphore_wait(bar, (NR - 1) + (NC - 1) + NR - home)
 
     def send_row(k, carry):
-        half, cc = lax.rem(k, 2), lax.rem(c + k // 2, NC)
+        half, cc = k & 1, (c + k // 2) & 7
         rr = 2 * c + half
 
         @pl.when(jnp.logical_or(rr != r, cc != c))
@@ -141,6 +153,8 @@
     def _():
         row_all[mine] = row_send[lax.rem(r, 2)]
 
+    for load in loads[3:]:
+        load.wait()
     for n, (w, f) in enumerate(((out_w, out_f), (in_w, in_f))):
         for b in range(5):
             weights[n, b] = w[:, b * 128 : b * 128 + 128].T
@@ -162,14 +176,14 @@
         col_copy(r, frm, csems.at[0], csems.at[1 + k]).wait_recv()
         col_copy(sibling, frm, csems.at[9], csems.at[10]).start()
 
-    load_pair.wait()
+    loads[2].wait()
 
     def turn(t, carry):
         block = jnp.concatenate([pair_in[t], pair_in[t + 16]], axis=0)
         pair[:, lanes(t, 128)] = block.T
         return carry
 
-    lax.fori_loop(0, 16, turn, 0)
+    lax.fori_loop(0, 16, turn, 0, unroll=8)
 
     @pl.when(home == 1)
     def _():
@@ -198,7 +212,7 @@
         outer[:, at] = jnp.dot(row_t[...], col_all[:, at], preferred_element_type=F32).astype(BF)
         return carry
 
-    lax.fori_loop(0, 8, outer_part, 0)
+    lax.fori_loop(0, 8, outer_part, 0, unroll=4)
 
     def opm(t2, carry):
         sides = []
@@ -219,16 +233,19 @@
         normed[:, at] = columns_normed(now).astype(BF)
         return carry
 
-    lax.fori_loop(0, 8, opm, 0)
-
-    def send_group(q, source, target, pairsems):
+    lax.fori_loop(0, 8, opm, 0, unroll=4)
+
+    def send_group(q, source, target, by_channel, pairsems):
         def one(k, carry):
-            rr, cc = q * 4 + k // NC, lax.rem(c + k, NC)
+            zz, cc = (z + k // NC) & 3, (c + k) & 7
+            rr = (q // 2) * 8 + zz * 2 + q % 2
 
             @pl.when(jnp.logical_or(rr != r, cc != c))
             def _():
                 pltpu.make_async_remote_copy(
-                    source.at[rr * NC + cc], target.at[me], pairsems.at[0], pairsems.at[1],
+                    source.at[q * 32 + zz * NC + cc if by_channel else rr * NC + cc],
+                    target.at[me if by_channel else channel],
+                    pairsems.at[0], pairsems.at[1],
                     device_id=(rr, cc), device_id_type=MESH,
                 ).start()
 
@@ -244,7 +261,7 @@
 
     def project(n, send, got, pairsems):
         def group(g, carry):
-            q = lax.rem(r // 4 + g, 4)
+            q = (group_here + g) & 3
             w = jnp.concatenate([weights[n, b, lanes(q, 32), :] for b in range(4)], axis=0)
             for m in range(4):
                 p = jnp.dot(w, normed[:, m * 512 : m * 512 + 512], preferred_element_type=F32)
@@ -258,18 +275,18 @@
             to = lanes(q, 32)
             send[to, 0] = spread_l[0:512, :].astype(BF).reshape(32, 16, 128)
             send[to, 1] = spread_r[0:512, :].astype(BF).reshape(32, 16, 128)
-            send_group(q, send, got, pairsems)
+            send_group(q, send, got, True, pairsems)
             return carry
 
         lax.fori_loop(0, 4, group, 0)
-        got[me] = send[me]
+        got[me] = send[channel]
 
         def gates(m, carry):
             at = lanes(m, 256)
             gate[:, at] = sigmoid(jnp.dot(weights[n, 4], normed[:, at], preferred_element_type=F32))
             return carry
 
-        lax.fori_loop(0, 8, gates, 0)
+        lax.fori_loop(0, 8, gates, 0, unroll=4)
         await_all(send, got, pairsems)
 
     def mix(n, got, back, target, pairsems):
@@ -282,25 +299,26 @@
                         matrices[f, to, m * 128 : m * 128 + 128] = both[h]
             return carry
 
-        lax.fori_loop(0, NR, place, 0)
+        lax.fori_loop(0, NR, place, 0, unroll=8)
         turned[...] = matrices[1 - n].T
 
         def group(g, carry):
-            q = lax.rem(r // 4 + g, 4)
-            at = lanes(q, 128)
-            left, right = (matrices[0, at, :], turned[...]) if n == 0 else (turned[at, :], matrices[1])
+            q = (group_here + g) & 3
+            first = (q // 2) * 8 + q % 2
+            rows, right = (matrices.at[0], turned[...]) if n == 0 else (turned, matrices[1])
+            left = jnp.concatenate([rows[lanes(first + 2 * k, 32), :] for k in range(4)], axis=0)
             mixed[...] = jnp.dot(left, right, preferred_element_type=F32)
             for k in range(4):
                 for m in range(4):
                     s = slice(m * 128, m * 128 + 128)
                     both = halves(mixed[k * 32 : k * 32 + 16, s], mixed[k * 32 + 16 : k * 32 + 32, s])
                     for h in range(2):
-                        back[(q * 4 + k) * NC + 2 * m + h] = both[h].astype(BF)
-            send_group(q, back, target, pairsems)
+                        back[(first + 2 * k) * NC + 2 * m + h] = both[h].astype(BF)
+            send_group(q, back, target, False, pairsems)
             return carry
 
         lax.fori_loop(0, 4, group, 0)
-        target[me] = back[me]
+        target[channel] = back[me]
         await_all(back, target, pairsems)
 
     def finish(n, mixed):
@@ -328,7 +346,7 @@
                     result[t2 * 2 + k + 16] = block[64:]
             return carry
 
-        lax.fori_loop(0, 8, one, 0)
+        lax.fori_loop(0, 8, one, 0, unroll=8)
 
     for n, (send, got, back, target) in enumerate(
         ((send1, got1, back1, mix1), (send2, got2, back2, mix2))
@@ -349,7 +367,7 @@
     incoming_final,
 ):
     vmem = pl.BlockSpec(memory_space=pltpu.VMEM)
-    anywhere = pl.BlockSpec(memory_space=pl.ANY)
+    hbm = pl.BlockSpec(memory_space=pltpu.HBM)
     v = pltpu.VMEM
     exchanged = [
         v((128, 2, 16, 128), BF), v((128, 2, 16, 128), BF), v((128, 16, 128), BF), v((128, 16, 128), BF),
@@ -357,16 +375,18 @@
     return pl.pallas_call(
         kernel,
         out_shape=jax.ShapeDtypeStruct((32, 64, 128), F32),
-        in_specs=[vmem, vmem, anywhere] + [vmem] * 5,
+        in_specs=[hbm] * 8,
         out_specs=vmem,
         scratch_shapes=[
+            v((16, 4096), BF), v((64, 64), BF), v((32, 64, 128), F32), v((1024, 128), BF),
+            v((128, 640), BF), v((128, 128), BF), v((128, 640), BF), v((128, 128), BF),
             v((2, 16, 1024), BF), v((256, 2048), BF), v((256, 1024), BF), v((1024, 256), BF),
-            v((1024, 2048), BF), v((32, 64, 128), F32), v((128, 2048), F32), v((128, 2048), BF),
+            v((1024, 2048), BF), v((128, 2048), F32), v((128, 2048), BF),
             v((128, 2048), F32), v((2048, 128), F32), v((2048, 128), F32),
             v((128, 1024), BF), v((2, 5, 128, 128), BF), v((2, 128, 128), BF),
             v((2, 512, 512), BF), v((512, 512), BF), v((128, 512), F32),
             *exchanged, *exchanged,
-            pltpu.SemaphoreType.DMA,
+            pltpu.SemaphoreType.DMA((8,)),
             pltpu.SemaphoreType.DMA((11,)),
             pltpu.SemaphoreType.DMA((2,)),
             pltpu.SemaphoreType.DMA((4, 2)),

time: 100 us -> 89 us (0.89)
  Pallas kernels: 97.8 us -> 86.5 us
    pallas_call x1, Pallas kernels: 97.8 us -> 86.5 us  [local(): pl.pallas_call(kernel, out_shape=jax.ShapeDtypeStruct((32, 64, 128), F32)...]
where the time goes in v2:
time: 89 us; the launch traced here: 88.9 us
  Pallas kernels  86.5 us (97%)
  local copies, waits for them, and re-layouts  2.31 us (3%)
    pallas_call x1, Pallas kernels, local(): pl.pallas_call(kernel, out_shape=jax.ShapeDtypeStruct((32, 64, 128), F32)...  86.5 us
    unnamed x1, local copies, waits for them, and re-layouts  2.31 us

profile of v2, /device:TPU:1, one launch (start us, length us, event | category | flops | bytes accessed | tf_op | source)
XLA Modules:
  0.0 88.9 jit_solution(8260423634265993040)
XLA Ops:
  0.0 86.5 %shard_map.82 = f32[32,64,128]{2,1,0:T(8,128)} custom-call(bf16[16,4096]{1,0:T(8,128)(2,1)} %align_hbm.1, bf16[64,64]{1,0:T(8,128)(2,1)} %factor_hbm.1, f32[32,64,128]{2,1,0:T(8,128)} %pair_hbm.1, bf16[1024,128]{1,0:T(8,128)(2,1)} %opm_hbm.1, bf16[128,640]{1,0:T(8,128)(2,1)} %out_w_hbm.1, bf16[128,128]{1,0:T(8,128)(2,1)} %out_f_hbm.1, ...), custom_call_target="tpu_custom_call" | custom-call | tf_op jit(solution)/shard_map/pallas_call | solution.py:375
  86.6 2.3 %copy.10 = f32[32,64,128]{2,1,0:T(8,128)} copy(f32[32,64,128]{2,1,0:T(8,128)} %shard_map.82) | data formatting | bytes 2097152

commit v3 on v2

--- a/solution.py
+++ b/solution.py
@@ -62,22 +62,25 @@
         load.start()
 
     def greet(rr, cc):
-        @pl.when(jnp.logical_or(rr != r, cc != c))
+        pl.semaphore_signal(bar, inc=1, device_id=(rr, cc), device_id_type=MESH)
+
+    def beside(k):
+        return (r // 8) * 8 + (z + k) % 4 * 2 + r % 2
+
+    sibling, across = r + 1 - 2 * (r % 2), (r + 8) % NR
+    for rr in (sibling, across, beside(1), beside(2), beside(3)):
+        greet(rr, c)
+
+    def greet_sources(k, carry):
+        rr = (r + k) & 15
+
+        @pl.when(jnp.logical_or(k > 0, home == 0))
         def _():
-            pl.semaphore_signal(bar, inc=1, device_id=(rr, cc), device_id_type=MESH)
-
-    def greet_rows(k, carry):
-        rr = (r + k) & 15
-        greet(rr, c)
-        greet(rr, r // 2)
-        return carry
-
-    def greet_cols(k, carry):
-        greet(r, (c + k) & 7)
-        return carry
-
-    lax.fori_loop(0, NR, greet_rows, 0)
-    lax.fori_loop(1, NC, greet_cols, 0)
+            greet(rr, r // 2)
+
+        return carry
+
+    lax.fori_loop(0, NR, greet_sources, 0)
 
     loads[0].wait()
     loads[1].wait()
@@ -119,9 +122,9 @@
                 [spread_l[pl.ds(at, 8, stride=128), :], spread_l[pl.ds(at + 64, 8, stride=128), :]], axis=0
             )
             piece = v if k == 0 else jnp.where(lane < 32 * k, piece, v)
-        row_send[n // 8, :, n % 8 * 128 : n % 8 * 128 + 128] = piece.astype(BF)
-
-    pl.semaphore_wait(bar, (NR - 1) + (NC - 1) + NR - home)
+        row_send[n // 8, n % 8] = piece.astype(BF)
+
+    pl.semaphore_wait(bar, 5 + NR - home)
 
     def send_row(k, carry):
         half, cc = k & 1, (c + k // 2) & 7
@@ -130,28 +133,28 @@
         @pl.when(jnp.logical_or(rr != r, cc != c))
         def _():
             pltpu.make_async_remote_copy(
-                row_send.at[half], row_all.at[mine], bsems.at[0], bsems.at[1],
+                row_send.at[half, cc], row_all.at[cc, mine], bsems.at[0], bsems.at[1],
                 device_id=(rr, cc), device_id_type=MESH,
             ).start()
 
         return carry
 
-    sibling = r + 1 - 2 * lax.rem(r, 2)
+    lax.fori_loop(0, NR, send_row, 0)
 
     def col_copy(rr, at, send_sem, got_sem):
         block = col_all.at[lanes(at, 16)]
         return pltpu.make_async_remote_copy(
-            block, block, send_sem, got_sem, device_id=(rr, c), device_id_type=MESH
+            block, block, csems.at[send_sem], csems.at[got_sem], device_id=(rr, c), device_id_type=MESH
         )
 
-    for k in range(1, 8):
-        col_copy(lax.rem(r + 2 * k, NR), r, csems.at[0], csems.at[1 + k]).start()
-    col_copy(sibling, r, csems.at[9], csems.at[10]).start()
-    lax.fori_loop(0, NR, send_row, 0)
+    col_copy(across, r, 0, 1).start()
+    for k in range(1, 4):
+        col_copy(beside(k), r, 0, 1 + k).start()
+    col_copy(sibling, r, 8, 9).start()
 
     @pl.when(home == 1)
     def _():
-        row_all[mine] = row_send[lax.rem(r, 2)]
+        row_all[c, mine] = row_send[r % 2, c]
 
     for load in loads[3:]:
         load.wait()
@@ -171,10 +174,29 @@
         )
         opm_w[:, q * 128 : q * 128 + 128] = block.T.astype(BF)
 
-    for k in range(1, 8):
-        frm = lax.rem(r + 16 - 2 * k, NR)
-        col_copy(r, frm, csems.at[0], csems.at[1 + k]).wait_recv()
-        col_copy(sibling, frm, csems.at[9], csems.at[10]).start()
+    col_copy(r, across, 0, 1).wait_recv()
+    for k in range(1, 4):
+        col_copy(beside(k), across, 0, 4 + k).start()
+    col_copy(sibling, across, 8, 9).start()
+
+    def await_rows(part):
+        pltpu.make_async_remote_copy(
+            part, part, bsems.at[0], bsems.at[1], device_id=(r, c), device_id_type=MESH
+        ).wait()
+
+    @pl.when(home == 1)
+    def _():
+        await_rows(row_all.at[0, pl.ds(0, 15 * 16)])
+
+    @pl.when(home == 0)
+    def _():
+        await_rows(row_all.at[0])
+
+    for k in range(1, NC):
+        part = row_all.at[c]
+        pltpu.make_async_remote_copy(
+            part, part, bsems.at[2], bsems.at[3], device_id=(r, (c + k) % NC), device_id_type=MESH
+        ).start()
 
     loads[2].wait()
 
@@ -185,26 +207,24 @@
 
     lax.fori_loop(0, 16, turn, 0, unroll=8)
 
-    @pl.when(home == 1)
-    def _():
-        part = row_all.at[pl.ds(0, 15 * 16)]
-        pltpu.make_async_remote_copy(
-            part, part, bsems.at[0], bsems.at[1], device_id=(r, c), device_id_type=MESH
-        ).wait()
-
-    @pl.when(home == 0)
-    def _():
-        pltpu.make_async_remote_copy(
-            row_all, row_all, bsems.at[0], bsems.at[1], device_id=(r, c), device_id_type=MESH
-        ).wait()
-
-    row_t[...] = row_all[...].T
+    for k in range(1, 4):
+        col_copy(r, beside(4 - k), 0, 1 + k).wait_recv()
+        col_copy(sibling, beside(4 - k), 8, 9).start()
+    for k in range(1, 4):
+        col_copy(r, beside(4 - k), 0, 4 + k).wait_recv()
+        col_copy(sibling, (beside(4 - k) + 8) % NR, 8, 9).start()
+    others = row_all.at[pl.ds(0, NC - 1)]
+    pltpu.make_async_remote_copy(
+        others, others, bsems.at[2], bsems.at[3], device_id=(r, c), device_id_type=MESH
+    ).wait()
+    for k in range(NC):
+        row_t[k * 128 : k * 128 + 128, :] = row_all[k].T
     seven, eight = col_all.at[pl.ds(0, 7 * 16)], col_all.at[pl.ds(0, 8 * 16)]
     pltpu.make_async_remote_copy(
         seven, seven, csems.at[0], csems.at[1], device_id=(r, c), device_id_type=MESH
     ).wait_send()
     pltpu.make_async_remote_copy(
-        eight, eight, csems.at[9], csems.at[10], device_id=(r, c), device_id_type=MESH
+        eight, eight, csems.at[8], csems.at[9], device_id=(r, c), device_id_type=MESH
     ).wait()
 
     def outer_part(n, carry):
@@ -235,32 +255,37 @@
 
     lax.fori_loop(0, 8, opm, 0, unroll=4)
 
-    def send_group(q, source, target, by_channel, pairsems):
-        def one(k, carry):
-            zz, cc = (z + k // NC) & 3, (c + k) & 7
-            rr = (q // 2) * 8 + zz * 2 + q % 2
-
-            @pl.when(jnp.logical_or(rr != r, cc != c))
-            def _():
-                pltpu.make_async_remote_copy(
-                    source.at[q * 32 + zz * NC + cc if by_channel else rr * NC + cc],
-                    target.at[me if by_channel else channel],
-                    pairsems.at[0], pairsems.at[1],
-                    device_id=(rr, cc), device_id_type=MESH,
-                ).start()
-
+    def row_of(q, zz):
+        return (q // 2) * 8 + zz * 2 + q % 2
+
+    def send_one(g, zz, cc, rr, source, target, phases):
+        pltpu.make_async_remote_copy(
+            source, target, phases.at[0], phases.at[1 + g], device_id=(rr, cc), device_id_type=MESH
+        ).start()
+
+    def await_phase(g, got, phases):
+        part = got.at[pl.ds(0, 31 if g == 0 else 32)]
+        pltpu.make_async_remote_copy(
+            part, part, phases.at[0], phases.at[1 + g], device_id=(r, c), device_id_type=MESH
+        ).wait_recv()
+
+    def await_sends(source, phases):
+        part = source.at[pl.ds(0, ND - 1)]
+        pltpu.make_async_remote_copy(
+            part, part, phases.at[0], phases.at[1], device_id=(r, c), device_id_type=MESH
+        ).wait_send()
+
+    def in_groups(group):
+        group(0)
+
+        def later(g, carry):
+            group(g)
             return carry
 
-        lax.fori_loop(0, 32, one, 0)
-
-    def await_all(source, target, pairsems):
-        pltpu.make_async_remote_copy(
-            source.at[pl.ds(0, ND - 1)], target.at[pl.ds(0, ND - 1)], pairsems.at[0], pairsems.at[1],
-            device_id=(r, c), device_id_type=MESH,
-        ).wait()
-
-    def project(n, send, got, pairsems):
-        def group(g, carry):
+        lax.fori_loop(1, 4, later, 0)
+
+    def project(n, send, got, phases):
+        def group(g):
             q = (group_here + g) & 3
             w = jnp.concatenate([weights[n, b, lanes(q, 32), :] for b in range(4)], axis=0)
             for m in range(4):
@@ -275,10 +300,15 @@
             to = lanes(q, 32)
             send[to, 0] = spread_l[0:512, :].astype(BF).reshape(32, 16, 128)
             send[to, 1] = spread_r[0:512, :].astype(BF).reshape(32, 16, 128)
-            send_group(q, send, got, True, pairsems)
-            return carry
-
-        lax.fori_loop(0, 4, group, 0)
+
+            def one(k, carry):
+                zz, cc = (z + k // NC) & 3, (c + k) & 7
+                send_one(g, zz, cc, row_of(q, zz), send.at[q * 32 + zz * NC + cc], got.at[me], phases)
+                return carry
+
+            lax.fori_loop(1 if isinstance(g, int) else 0, 32, one, 0, unroll=1)
+
+        in_groups(group)
         got[me] = send[channel]
 
         def gates(m, carry):
@@ -287,42 +317,61 @@
             return carry
 
         lax.fori_loop(0, 8, gates, 0, unroll=4)
-        await_all(send, got, pairsems)
-
-    def mix(n, got, back, target, pairsems):
-        def place(rr, carry):
-            for f in range(2):
-                for m in range(4):
-                    both = halves(got[rr * NC + 2 * m, f], got[rr * NC + 2 * m + 1, f])
-                    for h in range(2):
-                        to = pl.ds(pl.multiple_of(rr * 32 + h * 16, 16), 16)
-                        matrices[f, to, m * 128 : m * 128 + 128] = both[h]
-            return carry
-
-        lax.fori_loop(0, NR, place, 0, unroll=8)
-        turned[...] = matrices[1 - n].T
-
-        def group(g, carry):
+
+    def mix(n, send, got, before, back, target, phases):
+        for g in range(4):
+            source = (group_here - g) & 3
+            await_phase(g, got, before)
+            for zz in range(4):
+                rr = row_of(source, zz)
+                grouped = source * 128 + zz * 32
+                for f in range(2):
+                    start = rr * 32 if n == 0 and f == 1 else grouped
+                    for m in range(4):
+                        both = halves(got[rr * NC + 2 * m, f], got[rr * NC + 2 * m + 1, f])
+                        for h in range(2):
+                            to = pl.ds(pl.multiple_of(start + h * 16, 16), 16)
+                            matrices[f, to, m * 128 : m * 128 + 128] = both[h]
+            if n == 1:
+                turned[:, lanes(source, 128)] = matrices[0, lanes(source, 128), :].T
+        await_sends(send, before)
+
+        def group(g):
             q = (group_here + g) & 3
-            first = (q // 2) * 8 + q % 2
-            rows, right = (matrices.at[0], turned[...]) if n == 0 else (turned, matrices[1])
-            left = jnp.concatenate([rows[lanes(first + 2 * k, 32), :] for k in range(4)], axis=0)
-            mixed[...] = jnp.dot(left, right, preferred_element_type=F32)
+            if n == 0:
+                rows = [matrices[0, lanes(q * 4 + ((z + k) & 3), 32), :] for k in range(4)]
+            else:
+                rows = [turned[lanes(row_of(q, (z + k) & 3), 32), :] for k in range(4)]
+            left = jnp.concatenate(rows, axis=0)
+            if n == 0:
+                product = lax.dot_general(
+                    left, matrices[1], (((1,), (1,)), ((), ())), preferred_element_type=F32
+                )
+            else:
+                product = jnp.dot(left, matrices[1], preferred_element_type=F32)
             for k in range(4):
+                zz = (z + k) & 3
+                rr = row_of(q, zz)
                 for m in range(4):
                     s = slice(m * 128, m * 128 + 128)
-                    both = halves(mixed[k * 32 : k * 32 + 16, s], mixed[k * 32 + 16 : k * 32 + 32, s])
+                    both = halves(product[k * 32 : k * 32 + 16, s], product[k * 32 + 16 : k * 32 + 32, s])
                     for h in range(2):
-                        back[(first + 2 * k) * NC + 2 * m + h] = both[h].astype(BF)
-            send_group(q, back, target, False, pairsems)
-            return carry
-
-        lax.fori_loop(0, 4, group, 0)
+                        back[rr * NC + 2 * m + h] = both[h].astype(BF)
+                for i in range(NC):
+                    if k == 0 and i == 0 and isinstance(g, int):
+                        continue
+                    cc = (c + i) & 7
+                    send_one(g, zz, cc, rr, back.at[rr * NC + cc], target.at[channel], phases)
+
+        in_groups(group)
         target[channel] = back[me]
-        await_all(back, target, pairsems)
-
-    def finish(n, mixed):
-        spread_l[...] = mixed[...].astype(F32).reshape(2048, 128)
+
+    def finish(n, back, mixed, before):
+        for g in range(4):
+            source = (group_here - g) & 3
+            await_phase(g, mixed, before)
+            spread_l[lanes(source, 512), :] = mixed[lanes(source, 32)].astype(F32).reshape(512, 128)
+        await_sends(back, before)
 
         def one(t2, carry):
             sides = []
@@ -342,18 +391,23 @@
             else:
                 for k in range(2):
                     block = now[:, k * 128 : k * 128 + 128].T
-                    result[t2 * 2 + k] = block[:64]
-                    result[t2 * 2 + k + 16] = block[64:]
+                    pair_in[t2 * 2 + k] = block[:64]
+                    pair_in[t2 * 2 + k + 16] = block[64:]
+                for h in range(2):
+                    part = pl.ds(t2 * 2 + h * 16, 2)
+                    pltpu.make_async_copy(pair_in.at[part], result.at[part], lsem.at[0]).start()
             return carry
 
         lax.fori_loop(0, 8, one, 0, unroll=8)
+        if n == 1:
+            pltpu.make_async_copy(pair_in, result, lsem.at[0]).wait()
 
     for n, (send, got, back, target) in enumerate(
         ((send1, got1, back1, mix1), (send2, got2, back2, mix2))
     ):
         project(n, send, got, sems.at[2 * n])
-        mix(n, got, back, target, sems.at[2 * n + 1])
-        finish(n, target)
+        mix(n, send, got, sems.at[2 * n], back, target, sems.at[2 * n + 1])
+        finish(n, back, target, sems.at[2 * n + 1])
 
 
 def local(
@@ -376,20 +430,20 @@
         kernel,
         out_shape=jax.ShapeDtypeStruct((32, 64, 128), F32),
         in_specs=[hbm] * 8,
-        out_specs=vmem,
+        out_specs=hbm,
         scratch_shapes=[
             v((16, 4096), BF), v((64, 64), BF), v((32, 64, 128), F32), v((1024, 128), BF),
             v((128, 640), BF), v((128, 128), BF), v((128, 640), BF), v((128, 128), BF),
-            v((2, 16, 1024), BF), v((256, 2048), BF), v((256, 1024), BF), v((1024, 256), BF),
+            v((2, 8, 16, 128), BF), v((256, 2048), BF), v((8, 256, 128), BF), v((1024, 256), BF),
             v((1024, 2048), BF), v((128, 2048), F32), v((128, 2048), BF),
             v((128, 2048), F32), v((2048, 128), F32), v((2048, 128), F32),
             v((128, 1024), BF), v((2, 5, 128, 128), BF), v((2, 128, 128), BF),
             v((2, 512, 512), BF), v((512, 512), BF), v((128, 512), F32),
             *exchanged, *exchanged,
             pltpu.SemaphoreType.DMA((8,)),
-            pltpu.SemaphoreType.DMA((11,)),
-            pltpu.SemaphoreType.DMA((2,)),
-            pltpu.SemaphoreType.DMA((4, 2)),
+            pltpu.SemaphoreType.DMA((10,)),
+            pltpu.SemaphoreType.DMA((4,)),
+            pltpu.SemaphoreType.DMA((4, 5)),
         ],
         compiler_params=pltpu.CompilerParams(
             collective_id=0, has_side_effects=True, vmem_limit_bytes=56 << 20

time: 89 us -> 85.1 us (0.956)
  Pallas kernels: 86.5 us -> 82.6 us
    pallas_call x1, Pallas kernels: 86.5 us -> 82.6 us  [local(): pl.pallas_call(kernel, out_shape=jax.ShapeDtypeStruct((32, 64, 128), F32)...]
where the time goes in v3:
time: 85.1 us; the launch traced here: 84.9 us
  Pallas kernels  82.6 us (97%)
  local copies, waits for them, and re-layouts  2.31 us (3%)
    pallas_call x1, Pallas kernels, local(): pl.pallas_call(kernel, out_shape=jax.ShapeDtypeStruct((32, 64, 128), F32)...  82.6 us
    unnamed x1, local copies, waits for them, and re-layouts  2.31 us

profile of v3, /device:TPU:1, one launch (start us, length us, event | category | flops | bytes accessed | tf_op | source)
XLA Modules:
  0.0 84.9 jit_solution(17936282281701237630)
XLA Ops:
  0.0 82.6 %shard_map.82 = f32[32,64,128]{2,1,0:T(8,128)} custom-call(bf16[16,4096]{1,0:T(8,128)(2,1)} %align_hbm.1, bf16[64,64]{1,0:T(8,128)(2,1)} %factor_hbm.1, f32[32,64,128]{2,1,0:T(8,128)} %pair_hbm.1, bf16[1024,128]{1,0:T(8,128)(2,1)} %opm_hbm.1, bf16[128,640]{1,0:T(8,128)(2,1)} %out_w_hbm.1, bf16[128,128]{1,0:T(8,128)(2,1)} %out_f_hbm.1, ...), custom_call_target="tpu_custom_call" | custom-call | tf_op jit(solution)/shard_map/pallas_call | solution.py:429
  82.6 2.3 %copy.10 = f32[32,64,128]{2,1,0:T(8,128)} copy(f32[32,64,128]{2,1,0:T(8,128)} %shard_map.82) | data formatting | bytes 2097152

commit v4 on v3

--- a/solution.py
+++ b/solution.py
@@ -43,7 +43,7 @@
     align_hbm, factor_hbm, pair_hbm, opm_hbm, out_w_hbm, out_f_hbm, in_w_hbm, in_f_hbm, result,
     align_ref, factor_ref, pair_in, opm_ref, out_w, out_f, in_w, in_f, row_send, col_all, row_all, row_t, outer, pair, normed, gate, spread_l, spread_r,
     opm_w, weights, finals, matrices, turned, mixed,
-    send1, got1, back1, mix1, send2, got2, back2, mix2, lsem, csems, bsems, sems,
+    send1, got1, back1, mix1, send2, got2, back2, mix2, lsem, csems, bsems, rsems, sems,
 ):
     r, c = position()
     me = r * NC + c
@@ -192,11 +192,23 @@
     def _():
         await_rows(row_all.at[0])
 
-    for k in range(1, NC):
-        part = row_all.at[c]
-        pltpu.make_async_remote_copy(
-            part, part, bsems.at[2], bsems.at[3], device_id=(r, (c + k) % NC), device_id_type=MESH
-        ).start()
+    over = c + 1 - 2 * (c % 2)
+
+    def aside(k):
+        return (c + 2 * k) % NC
+
+    def row_copy(cc, half, at, send_sem, got_sem):
+        part = row_all.at[at, pl.ds(half * 128, 128)]
+        return pltpu.make_async_remote_copy(
+            part, part, rsems.at[send_sem], rsems.at[got_sem], device_id=(r, cc), device_id_type=MESH
+        )
+
+    row_copy(over, 0, c, 0, 2).start()
+    for k in range(1, 4):
+        row_copy(aside(k), 1, c, 1, 3 + k).start()
+    for k in range(1, 4):
+        row_copy(aside(k), 0, c, 0, 3).start()
+    row_copy(over, 1, c, 1, 7).start()
 
     loads[2].wait()
 
@@ -207,16 +219,28 @@
 
     lax.fori_loop(0, 16, turn, 0, unroll=8)
 
+    row_copy(c, 0, over, 0, 2).wait_recv()
+    for k in range(1, 4):
+        row_copy(aside(k), 0, over, 0, 3).start()
+    for k in range(1, 4):
+        row_copy(c, 1, aside(4 - k), 1, 3 + k).wait_recv()
+        row_copy(over, 1, aside(4 - k), 1, 7).start()
     for k in range(1, 4):
         col_copy(r, beside(4 - k), 0, 1 + k).wait_recv()
         col_copy(sibling, beside(4 - k), 8, 9).start()
     for k in range(1, 4):
         col_copy(r, beside(4 - k), 0, 4 + k).wait_recv()
         col_copy(sibling, (beside(4 - k) + 8) % NR, 8, 9).start()
-    others = row_all.at[pl.ds(0, NC - 1)]
-    pltpu.make_async_remote_copy(
-        others, others, bsems.at[2], bsems.at[3], device_id=(r, c), device_id_type=MESH
-    ).wait()
+    def row_blocks(count, send_sem, got_sem):
+        part = row_all.at[pl.ds(0, count), pl.ds(0, 128)]
+        return pltpu.make_async_remote_copy(
+            part, part, rsems.at[send_sem], rsems.at[got_sem], device_id=(r, c), device_id_type=MESH
+        )
+
+    row_blocks(6, 0, 3).wait_recv()
+    row_blocks(4, 1, 7).wait_recv()
+    row_blocks(7, 0, 3).wait_send()
+    row_blocks(7, 1, 7).wait_send()
     for k in range(NC):
         row_t[k * 128 : k * 128 + 128, :] = row_all[k].T
     seven, eight = col_all.at[pl.ds(0, 7 * 16)], col_all.at[pl.ds(0, 8 * 16)]
@@ -227,12 +251,9 @@
         eight, eight, csems.at[8], csems.at[9], device_id=(r, c), device_id_type=MESH
     ).wait()
 
-    def outer_part(n, carry):
-        at = lanes(n, 256)
-        outer[:, at] = jnp.dot(row_t[...], col_all[:, at], preferred_element_type=F32).astype(BF)
-        return carry
-
-    lax.fori_loop(0, 8, outer_part, 0, unroll=4)
+    for k in range(4):
+        at = slice(k * 256, k * 256 + 256)
+        outer[at, :] = jnp.dot(row_t[at, :], col_all[...], preferred_element_type=F32).astype(BF)
 
     def opm(t2, carry):
         sides = []
@@ -442,7 +463,8 @@
             *exchanged, *exchanged,
             pltpu.SemaphoreType.DMA((8,)),
             pltpu.SemaphoreType.DMA((10,)),
-            pltpu.SemaphoreType.DMA((4,)),
+            pltpu.SemaphoreType.DMA((2,)),
+            pltpu.SemaphoreType.DMA((8,)),
             pltpu.SemaphoreType.DMA((4, 5)),
         ],
         compiler_params=pltpu.CompilerParams(

time: 85.1 us -> 83.4 us (0.980)
  Pallas kernels: 82.6 us -> 80.9 us
    pallas_call x1, Pallas kernels: 82.6 us -> 80.9 us  [local(): pl.pallas_call(kernel, out_shape=jax.ShapeDtypeStruct((32, 64, 128), F32)...]
where the time goes in v4:
time: 83.4 us; the launch traced here: 83.2 us
  Pallas kernels  80.9 us (97%)
  local copies, waits for them, and re-layouts  2.31 us (3%)
    pallas_call x1, Pallas kernels, local(): pl.pallas_call(kernel, out_shape=jax.ShapeDtypeStruct((32, 64, 128), F32)...  80.9 us
    unnamed x1, local copies, waits for them, and re-layouts  2.31 us

profile of v4, /device:TPU:1, one launch (start us, length us, event | category | flops | bytes accessed | tf_op | source)
XLA Modules:
  0.0 83.2 jit_solution(14755754494202000347)
XLA Ops:
  0.0 80.9 %shard_map.82 = f32[32,64,128]{2,1,0:T(8,128)} custom-call(bf16[16,4096]{1,0:T(8,128)(2,1)} %align_hbm.1, bf16[64,64]{1,0:T(8,128)(2,1)} %factor_hbm.1, f32[32,64,128]{2,1,0:T(8,128)} %pair_hbm.1, bf16[1024,128]{1,0:T(8,128)(2,1)} %opm_hbm.1, bf16[128,640]{1,0:T(8,128)(2,1)} %out_w_hbm.1, bf16[128,128]{1,0:T(8,128)(2,1)} %out_f_hbm.1, ...), custom_call_target="tpu_custom_call" | custom-call | tf_op jit(solution)/shard_map/pallas_call | solution.py:450
  80.9 2.3 %copy.10 = f32[32,64,128]{2,1,0:T(8,128)} copy(f32[32,64,128]{2,1,0:T(8,128)} %shard_map.82) | data formatting | bytes 2097152

commit v5 on v4

--- a/solution.py
+++ b/solution.py
@@ -274,7 +274,7 @@
         normed[:, at] = columns_normed(now).astype(BF)
         return carry
 
-    lax.fori_loop(0, 8, opm, 0, unroll=4)
+    lax.fori_loop(0, 8, opm, 0, unroll=8)
 
     def row_of(q, zz):
         return (q // 2) * 8 + zz * 2 + q % 2

time: 83.4 us -> 82.3 us (0.987)
  Pallas kernels: 80.9 us -> 79.8 us
    pallas_call x1, Pallas kernels: 80.9 us -> 79.8 us  [local(): pl.pallas_call(kernel, out_shape=jax.ShapeDtypeStruct((32, 64, 128), F32)...]
where the time goes in v5:
time: 82.3 us; the launch traced here: 82.2 us
  Pallas kernels  79.8 us (97%)
  local copies, waits for them, and re-layouts  2.31 us (3%)
    pallas_call x1, Pallas kernels, local(): pl.pallas_call(kernel, out_shape=jax.ShapeDtypeStruct((32, 64, 128), F32)...  79.8 us
    unnamed x1, local copies, waits for them, and re-layouts  2.31 us

profile of v5, /device:TPU:1, one launch (start us, length us, event | category | flops | bytes accessed | tf_op | source)
XLA Modules:
  0.0 82.2 jit_solution(10556978843169760219)
XLA Ops:
  0.0 79.8 %shard_map.82 = f32[32,64,128]{2,1,0:T(8,128)} custom-call(bf16[16,4096]{1,0:T(8,128)(2,1)} %align_hbm.1, bf16[64,64]{1,0:T(8,128)(2,1)} %factor_hbm.1, f32[32,64,128]{2,1,0:T(8,128)} %pair_hbm.1, bf16[1024,128]{1,0:T(8,128)(2,1)} %opm_hbm.1, bf16[128,640]{1,0:T(8,128)(2,1)} %out_w_hbm.1, bf16[128,128]{1,0:T(8,128)(2,1)} %out_f_hbm.1, ...), custom_call_target="tpu_custom_call" | custom-call | tf_op jit(solution)/shard_map/pallas_call | solution.py:450
  79.8 2.3 %copy.10 = f32[32,64,128]{2,1,0:T(8,128)} copy(f32[32,64,128]{2,1,0:T(8,128)} %shard_map.82) | data formatting | bytes 2097152

commit v6 on v5

--- a/solution.py
+++ b/solution.py
@@ -327,7 +327,7 @@
                 send_one(g, zz, cc, row_of(q, zz), send.at[q * 32 + zz * NC + cc], got.at[me], phases)
                 return carry
 
-            lax.fori_loop(1 if isinstance(g, int) else 0, 32, one, 0, unroll=1)
+            lax.fori_loop(1 if isinstance(g, int) else 0, 32, one, 0, unroll=4)
 
         in_groups(group)
         got[me] = send[channel]

time: 82.3 us -> 81.9 us (level)
  no operation moved by 1% of the time
where the time goes in v6:
time: 81.9 us; the launch traced here: 81.8 us
  Pallas kernels  79.5 us (97%)
  local copies, waits for them, and re-layouts  2.31 us (3%)
    pallas_call x1, Pallas kernels, local(): pl.pallas_call(kernel, out_shape=jax.ShapeDtypeStruct((32, 64, 128), F32)...  79.5 us
    unnamed x1, local copies, waits for them, and re-layouts  2.31 us

profile of v6, /device:TPU:1, one launch (start us, length us, event | category | flops | bytes accessed | tf_op | source)
XLA Modules:
  0.0 81.8 jit_solution(10656637729173674334)
XLA Ops:
  0.0 79.5 %shard_map.82 = f32[32,64,128]{2,1,0:T(8,128)} custom-call(bf16[16,4096]{1,0:T(8,128)(2,1)} %align_hbm.1, bf16[64,64]{1,0:T(8,128)(2,1)} %factor_hbm.1, f32[32,64,128]{2,1,0:T(8,128)} %pair_hbm.1, bf16[1024,128]{1,0:T(8,128)(2,1)} %opm_hbm.1, bf16[128,640]{1,0:T(8,128)(2,1)} %out_w_hbm.1, bf16[128,128]{1,0:T(8,128)(2,1)} %out_f_hbm.1, ...), custom_call_target="tpu_custom_call" | custom-call | tf_op jit(solution)/shard_map/pallas_call | solution.py:450
  79.5 2.3 %copy.10 = f32[32,64,128]{2,1,0:T(8,128)} copy(f32[32,64,128]{2,1,0:T(8,128)} %shard_map.82) | data formatting | bytes 2097152
